TPU v7x, 512 devices: a whole 4x8x8 slice. The times are simulated.
512 devices in a mesh: group: 16 (over x_lo, z), dev: 32 (over x_hi, y, core).
Axes of the slice: x: 4 (x_hi: 2, x_lo: 2; x = x_hi * 2 + x_lo), y: 8, z: 8, core: 2. Of those that a mesh axis runs over, the one named last changes fastest.
Arguments:
- patches: bfloat16 [16, 32, 256, 1152], P('group', 'dev'), may hold values from -6 to 6
- norm_gain: float32 [1152], replicated, may hold values from 0.1 to 1.9
- kv_weight: bfloat16 [4096, 1152], P(('group', 'dev')), may hold values from -0.1875 to 0.1875
- latent_q: bfloat16 [64, 2048], replicated
- clip_frames: int32 [16, 32], P('group', 'dev'), may hold values from 1 to 8, as said below
- row_owner: int32 [16, 32, 256], P('group', 'dev'), may hold values from 0 to 31, as said below
- row_slot: int32 [16, 32, 256], P('group', 'dev'), may hold values from 0 to 15, as said below
- slot_pos: int32 [16, 32, 512], P('group', 'dev'), may hold values from 0 to 512, as said below
- latent_blocks: int32 [16, 32, 64, 2], P('group', 'dev'), may hold values from -1 to 3, as said below
Outputs:
- latent_out: bfloat16 [2048, 32768], P('dev', 'group')
Inputs may be any that keep to these rules, and one draw needn't show every extreme that they name: `clip_frames`: A group's clips hold 4 * 32 frames together; every group has a clip of 8 frames and one of 2 frames or fewer. `row_owner`: A device holds exactly f * 2 rows of each clip of its group that has f frames. `row_slot`: the rows that one device holds for one clip carry the slots 0, 1, and so on, each once. `slot_pos`: for a clip of f frames the entries s * 16 + k, with k below the number of rows of that clip on device s, name the positions 0 to f * 64 - 1 each once; every other entry is 512. `latent_blocks`: for a clip of b = ceil(f / 2) blocks, entry 0 of latent i is block i * b // 64; entry 1 is a block beside it, or -1 where b is 1.
All inputs are finite; a program needn't handle non-finite values.
Results may differ from a plain program's by a relative error of at most 0.0055.
The roundings to bfloat16 on the way count: a program that leaves them out, or rounds other values in their place, can miss the bound.
Values may be sent and summed in bfloat16 or wider, within the bound.
A program may use at most 64 MiB of HBM per device.

v0:
```python
import jax
import jax.numpy as jnp
from jax import lax
from jax.sharding import PartitionSpec as P

HD = 128
LAT = 64
FR_ROWS = 64


def rms_rows(patch_rows, norm_gain):
    widened = patch_rows.astype(jnp.float32)
    inverse_rms = lax.rsqrt(jnp.mean(widened * widened, axis=-1, keepdims=True) + 1e-06)
    return (widened * inverse_rms * norm_gain).astype(jnp.bfloat16)


def product_rows(input_rows, weight_piece):
    return lax.dot_general(
        input_rows, weight_piece, (((1,), (1,)), ((), ())), preferred_element_type=jnp.float32
    )


def project(input_rows, kv_weight, live_rows):
    block_rows = 2 * FR_ROWS
    block_count = input_rows.shape[0] // block_rows
    weight_piece = lax.all_gather(kv_weight, ("group", "dev"), axis=0, tiled=True)
    outputs = []
    for block in range(block_count):
        rows_here = input_rows[block * block_rows : (block + 1) * block_rows]
        empty = jnp.zeros((block_rows, weight_piece.shape[0]), jnp.float32)
        outputs.append(
            lax.cond(
                block * block_rows < live_rows,
                lambda: product_rows(rows_here, weight_piece),
                lambda: empty,
            )
        )
    projected = jnp.concatenate(outputs, axis=0)
    return projected.astype(jnp.bfloat16)


def attend(keyval, frames, listed, latent_q):
    capacity = keyval.shape[0]
    kv_width = keyval.shape[1] // 2
    head_count = kv_width // HD
    key_part = keyval[:, :kv_width].reshape(capacity, head_count, HD)
    value_part = keyval[:, kv_width:].reshape(capacity, head_count, HD)
    queries = latent_q.reshape(LAT, head_count, HD)
    scores = jnp.einsum(
        "ihd,jhd->hij", queries, key_part, preferred_element_type=jnp.float32
    ) * HD ** (-0.5)
    position = jnp.arange(capacity, dtype=jnp.int32)
    block_id = position // (2 * FR_ROWS)
    allowed = ((block_id[None, :] == listed[:, 0:1]) | (block_id[None, :] == listed[:, 1:2])) & (
        position[None, :] < frames * FR_ROWS
    )
    scores = jnp.where(allowed[None, :, :], scores, jnp.float32(-1e30))
    row_max = jnp.max(scores, axis=-1, keepdims=True)
    raised = jnp.exp(scores - row_max)
    row_sum = jnp.sum(raised, axis=-1, keepdims=True)
    attn_weights = (raised / row_sum).astype(jnp.bfloat16)
    blended = jnp.einsum(
        "hij,jhd->hdi", attn_weights, value_part, preferred_element_type=jnp.float32
    )
    return blended.astype(jnp.bfloat16).reshape(kv_width, LAT)


def per_device(
    patches,
    norm_gain,
    kv_weight,
    latent_q,
    clip_frames,
    row_owner,
    row_slot,
    slot_pos,
    latent_blocks,
):
    dev_count = lax.axis_size("dev")
    normed = rms_rows(patches[0, 0], norm_gain)
    places = slot_pos[0, 0]
    capacity = places.shape[0]
    slot_count = capacity // dev_count
    target = row_owner[0, 0] * slot_count + row_slot[0, 0]
    frames = clip_frames[0, 0]
    outbox = jnp.zeros((capacity, normed.shape[1]), jnp.bfloat16).at[target].set(normed)
    received = lax.all_to_all(
        outbox.reshape(dev_count, slot_count, normed.shape[1]),
        "dev",
        split_axis=0,
        concat_axis=0,
        tiled=True,
    )
    timeline = (
        jnp.zeros_like(outbox)
        .at[places]
        .set(received.reshape(capacity, normed.shape[1]), mode="drop")
    )
    keyval = project(timeline, kv_weight, frames * FR_ROWS)
    blended = attend(keyval, frames, latent_blocks[0, 0], latent_q)
    return lax.all_to_all(blended, "dev", split_axis=0, concat_axis=1, tiled=True)


def solution(mesh):
    return jax.shard_map(
        per_device,
        mesh=mesh,
        in_specs=(
            P("group", "dev", None, None),
            P(),
            P(("group", "dev"), None),
            P(),
            P("group", "dev"),
            P("group", "dev", None),
            P("group", "dev", None),
            P("group", "dev", None),
            P("group", "dev", None, None),
        ),
        out_specs=P("dev", "group"),
        check_vma=False,
    )
```

profile of v0, /device:TPU:1, one launch (start us, length us, event | category | flops | bytes accessed | tf_op | source)
XLA Modules:
  0.0 911.5 jit_solution(12294368740215103621)
XLA Ops:
  6.5 0.7 all-gather.2.cloned.1.call-update
  7.3 1.3 fusion.10
  8.6 0.7 compare_select_fusion.1
  9.3 3.3 scatter_custom_fusion
  12.6 11.2 %all-to-all-start = ((bf16[32,16,1152]{2,1,0:T(8,128)(2,1)}), bf16[32,16,1152]{2,1,0:T(8,128)(2,1)S(1)}, u32[]{:S(2)}, u32[]{:S(2)}) async-start(bf16[32,16,1152]{2,1,0:T(8,128)(2,1)} %bitcast.7), calls=%async_computation | async-start | bytes 2359296 | tf_op jit(solution)/shard_map/all_to_all | solution.py:87
  24.5 0.7 or_and_fusion
  25.3 29.3 %all-to-all-done = bf16[32,16,1152]{2,1,0:T(8,128)(2,1)S(1)} async-done(((bf16[32,16,1152]{2,1,0:T(8,128)(2,1)}), bf16[32,16,1152]{2,1,0:T(8,128)(2,1)S(1)}, u32[]{:S(2)}, u32[]{:S(2)}) %all-to-all-start) | async-done | bytes 1179680 | tf_op jit(solution)/shard_map/all_to_all | solution.py:87
  54.6 3.1 scatter_custom_fusion.1
  57.7 779.5 %all-gather.2.cloned.1.call-done = bf16[4096,1152]{1,0:T(8,128)(2,1)} async-done(((bf16[8,1152]{1,0:T(8,128)(2,1)}), bf16[4096,1152]{1,0:T(8,128)(2,1)}) %all-gather.2.cloned.1.call-update) | async-done | bytes 9437200 | tf_op jit(solution)/shard_map/all_gather | solution.py:26
  837.2 6.8 conditional.4
  837.2 6.8 fusion
  844.0 0.7 copy.28
  844.8 1.3 copy.29
  846.2 1.3 copy.30
  847.8 1.3 copy.31
  849.1 1.8 pad_maximum_fusion
  850.9 1.6 fusion.37
  852.5 0.4 fusion.24
  853.3 0.7 fusion.38
  854.0 3.5 convolution_convert_fusion
  858.1 0.4 reshape.211
  858.5 44.8 %all_to_all.24 = bf16[32,2,2048]{2,1,0:T(2,128)(2,1)S(1)} all-to-all(bf16[32,2,2048]{2,1,0:T(2,128)(2,1)S(1)} %reshape.211), channel_id=1, replica_groups=mesh['group'=16,'dev'=32] {'dev'}, dimensions={0} | all-to-all | bytes 524288 | tf_op jit(solution)/shard_map/all_to_all | solution.py:101
  903.3 0.4 reshape.212
  903.7 0.9 copy.40
  (25 shorter events, 1.8 us)
Async XLA Ops:
  6.5 846.0 %copy-start = (bf16[64,2048]{1,0:T(8,128)(2,1)S(1)}, bf16[64,2048]{1,0:T(8,128)(2,1)}, u32[]{:S(2)}) copy-start(bf16[64,2048]{1,0:T(8,128)(2,1)} %param.20) | copy-start | bytes 786436
  6.5 830.7 %all-gather.2.cloned.1.call-start = ((), (), s32[]{:S(2)}) async-start(), calls=%async_computation.2 | async-start | bytes 9455616 | tf_op jit(solution)/shard_map/all_gather | solution.py:26
  8.5 16.0 %copy-start.4 = (s32[1,1,64,2]{2,3,1,0:T(2,128)S(1)}, s32[1,1,64,2]{2,3,1,0:T(2,128)}, u32[]{:S(2)}) copy-start(s32[1,1,64,2]{2,3,1,0:T(2,128)} %param.25) | copy-start | bytes 1540
  8.5 16.0 %copy-start.3 = (s32[1,1,512]{2,1,0:T(1,128)S(1)}, s32[1,1,512]{2,1,0:T(1,128)}, u32[]{:S(2)}) copy-start(s32[1,1,512]{2,1,0:T(1,128)} %param.24) | copy-start | bytes 6148
  12.6 42.0 %all-to-all-start = ((bf16[32,16,1152]{2,1,0:T(8,128)(2,1)}), bf16[32,16,1152]{2,1,0:T(8,128)(2,1)S(1)}, u32[]{:S(2)}, u32[]{:S(2)}) async-start(bf16[32,16,1152]{2,1,0:T(8,128)(2,1)} %bitcast.7), calls=%async_computation | async-start | bytes 2359296 | tf_op jit(solution)/shard_map/all_to_all | solution.py:87
  847.8 1.3 copy-start.1
  852.5 0.8 copy-start.2
Sparse Core Ops, SparseCore 0:
  9.6 827.5 all-gather.1
where the time goes:
time: 912 us; the launch traced here: 911 us
  waiting for transfers between devices  810 us (89%)
  blocking collectives  44.8 us (5%)
  between operations  14.2 us (2%)
  local copies, waits for them, and re-layouts  12.1 us (1%)
  starting transfers between devices  11.2 us (1%)
  matrix products  10.7 us (1%)
    all_gather x1, waiting for transfers between devices, project(): lax.all_gather(kv_weight, ('group', 'dev'), axis=0, tiled=True)  780 us
    all_to_all x1, blocking collectives, per_device(): lax.all_to_all(blended, 'dev', split_axis=0, concat_axis=1, tiled=True)  44.8 us
    all_to_all x1, waiting for transfers between devices, per_device(): lax.all_to_all(outbox.reshape(dev_count, slot_count, normed.shape[1]), 'd...  29.3 us
  transfers between devices with their start and end apart: 2, of which 2 were waited for; matrix products, arithmetic and copies ran while one was open for 1% of the time, Pallas kernels for 0%

commit v1 on v0

--- a/solution.py
+++ b/solution.py
@@ -23,7 +23,8 @@
 def project(input_rows, kv_weight, live_rows):
     block_rows = 2 * FR_ROWS
     block_count = input_rows.shape[0] // block_rows
-    weight_piece = lax.all_gather(kv_weight, ("group", "dev"), axis=0, tiled=True)
+    outgoing = jnp.stack([kv_weight] * lax.axis_size(("group", "dev")))
+    weight_piece = jnp.concatenate(lax.all_to_all(outgoing, ("group", "dev"), 0, 0), axis=0)
     outputs = []
     for block in range(block_count):
         rows_here = input_rows[block * block_rows : (block + 1) * block_rows]

time: 912 us -> 344 us (0.38)
  waiting for transfers between devices: 810 us -> 205 us
  blocking collectives: 44.8 us -> 85.8 us
  between operations: 14.2 us -> 0.85 us
    all_gather x1 -> x0, waiting for transfers between devices: 780 us -> none  [project(): lax.all_gather(kv_weight, ('group', 'dev'), axis=0, tiled=True)]
    all_to_all x1, waiting for transfers between devices: 29.3 us -> 205 us  [project(): lax.all_to_all(outgoing, ('group', 'dev'), 0, 0)]
    all_to_all x0 -> x1, blocking collectives: none -> 44.1 us  [per_device(): lax.all_to_all(outbox.reshape(dev_count, slot_count, normed.shape[1]), 'd...]
  transfers between devices with their start and end apart: 2 -> 1, of which waited for: 2 -> 1; matrix products, arithmetic and copies ran while one was open for 1% -> 1% of each run, Pallas kernels for 0% -> 0%
where the time goes in v1:
time: 344 us; the launch traced here: 343 us
  waiting for transfers between devices  205 us (60%)
  blocking collectives  85.8 us (25%)
  local copies, waits for them, and re-layouts  16.5 us (5%)
  starting transfers between devices  16.5 us (5%)
  matrix products  10.7 us (3%)
  other arithmetic  7.81 us (2%)
    all_to_all x1, waiting for transfers between devices, project(): lax.all_to_all(outgoing, ('group', 'dev'), 0, 0)  205 us
    all_to_all x1, blocking collectives, per_device(): lax.all_to_all(outbox.reshape(dev_count, slot_count, normed.shape[1]), 'd...  44.1 us
    all_to_all x1, blocking collectives, per_device(): lax.all_to_all(blended, 'dev', split_axis=0, concat_axis=1, tiled=True)  41.7 us
    all_to_all x1, starting transfers between devices, project(): lax.all_to_all(outgoing, ('group', 'dev'), 0, 0)  16.5 us
  transfers between devices with their start and end apart: 1, of which 1 were waited for; matrix products, arithmetic and copies ran while one was open for 1% of the time, Pallas kernels for 0%

profile of v1, /device:TPU:1, one launch (start us, length us, event | category | flops | bytes accessed | tf_op | source)
XLA Modules:
  0.0 342.9 jit_solution(15000831957269959481)
XLA Ops:
  0.0 1.3 fusion.10
  1.3 0.7 compare_select_fusion.1
  2.0 2.6 scatter_custom_fusion
  4.6 44.1 %all_to_all.29 = bf16[32,16,1152]{2,1,0:T(8,128)(2,1)S(1)} all-to-all(bf16[32,16,1152]{2,1,0:T(8,128)(2,1)S(1)} %bitcast.58), channel_id=1, replica_groups=mesh['group'=16,'dev'=32] {'dev'}, dimensions={0} | all-to-all | bytes 2359296 | tf_op jit(solution)/shard_map/all_to_all | solution.py:88
  48.7 4.3 %stack.2 = bf16[512,8,1152]{2,1,0:T(8,128)(2,1)} broadcast(bf16[8,1152]{1,0:T(8,128)(2,1)S(1)} %copy-done.3), dimensions={1,2} | broadcast | bytes 9455616 | tf_op jit(solution)/shard_map/stack | solution.py:26
  53.1 16.5 %all-to-all-start.1 = ((bf16[512,8,1152]{2,1,0:T(8,128)(2,1)}), bf16[512,8,1152]{2,1,0:T(8,128)(2,1)}, u32[]{:S(2)}, u32[]{:S(2)}) async-start(bf16[512,8,1152]{2,1,0:T(8,128)(2,1)} %stack.2), calls=%async_computation.1 | async-start | bytes 18874368 | tf_op jit(solution)/shard_map/all_to_all | solution.py:27
  70.3 0.7 or_and_fusion
  71.0 3.1 scatter_custom_fusion.1
  74.1 204.6 %all-to-all-done.1 = bf16[512,8,1152]{2,1,0:T(8,128)(2,1)} async-done(((bf16[512,8,1152]{2,1,0:T(8,128)(2,1)}), bf16[512,8,1152]{2,1,0:T(8,128)(2,1)}, u32[]{:S(2)}, u32[]{:S(2)}) %all-to-all-start.1) | async-done | bytes 9437216 | tf_op jit(solution)/shard_map/all_to_all | solution.py:27
  278.6 6.8 %conditional.4 = (bf16[128,4096]{1,0:T(8,128)(2,1)S(1)}) conditional(s32[]{:T(128)} %convert_element_type.28, () %tuple.29, (bf16[512,1152]{1,0:T(8,128)(2,1)S(1)}, bf16[4096,1152]{1,0:T(8,128)(2,1)}) %tuple.30), branch_computations={%region_3.0_spmd, %region_4.0_spmd} | conditional | flops 1207959552 | bytes 10780680 | solution.py:33
  278.6 6.8 %fusion = bf16[128,4096]{1,0:T(8,128)(2,1)S(1)} fusion(bf16[4096,1152]{1,0:T(8,128)(2,1)} %get-tuple-element.38, bf16[512,1152]{1,0:T(8,128)(2,1)S(1)} %get-tuple-element.37), kind=kOutput, calls=%fused_computation.2 | convolution fusion | flops 1207959552 | bytes 10780672 | tf_op jit(solution)/shard_map/cond/branch_1_fun/dot_general | solution.py:18
  285.4 0.7 copy.28
  286.4 1.3 copy.29
  287.8 1.3 copy.30
  289.3 1.3 copy.31
  290.6 1.8 pad_maximum_fusion
  292.4 1.6 fusion.37
  294.0 0.4 fusion.24
  294.8 0.7 fusion.38
  295.5 3.5 %convolution_convert_fusion = bf16[16,128,64]{1,2,0:T(8,128)(2,1)S(1)} fusion(bf16[512,16,128]{0,2,1:T(8,128)(2,1)} %bitcast.61, f32[16,64]{1,0:T(8,128)S(1)} %fusion.38, f32[16,512,64]{1,2,0:T(8,128)S(1)} %fusion.24, pred[64,512]{1,0:T(8,128)(4,1)S(1)} %copy-done.2), kind=kOutput, calls=%fused_computation.18 | convolution fusion | flops 136971776 | bytes 4493312 | tf_op jit(solution)/shard_map/hij,jhd->hdi/dot_general | solution.py:63
  299.6 0.4 reshape.217
  300.0 41.7 %all_to_all.30 = bf16[32,2,2048]{2,1,0:T(2,128)(2,1)S(1)} all-to-all(bf16[32,2,2048]{2,1,0:T(2,128)(2,1)S(1)} %reshape.217), channel_id=1, replica_groups=mesh['group'=16,'dev'=32] {'dev'}, dimensions={0} | all-to-all | bytes 524288 | tf_op jit(solution)/shard_map/all_to_all | solution.py:102
  341.7 0.4 reshape.218
  342.0 0.9 copy.40
  (26 shorter events, 1.8 us)
Async XLA Ops:
  0.0 294.0 %copy-start = (bf16[64,2048]{1,0:T(8,128)(2,1)S(1)}, bf16[64,2048]{1,0:T(8,128)(2,1)}, u32[]{:S(2)}) copy-start(bf16[64,2048]{1,0:T(8,128)(2,1)} %param.20) | copy-start | bytes 786436
  1.3 47.4 %copy-start.3 = (bf16[8,1152]{1,0:T(8,128)(2,1)S(1)}, bf16[8,1152]{1,0:T(8,128)(2,1)}, u32[]{:S(2)}) copy-start(bf16[8,1152]{1,0:T(8,128)(2,1)} %param.19) | copy-start | bytes 55300
  53.1 17.2 %copy-start.5 = (s32[1,1,64,2]{2,3,1,0:T(2,128)S(1)}, s32[1,1,64,2]{2,3,1,0:T(2,128)}, u32[]{:S(2)}) copy-start(s32[1,1,64,2]{2,3,1,0:T(2,128)} %param.25) | copy-start | bytes 1540
  53.1 17.2 %copy-start.4 = (s32[1,1,512]{2,1,0:T(1,128)S(1)}, s32[1,1,512]{2,1,0:T(1,128)}, u32[]{:S(2)}) copy-start(s32[1,1,512]{2,1,0:T(1,128)} %param.24) | copy-start | bytes 6148
  53.1 225.6 %all-to-all-start.1 = ((bf16[512,8,1152]{2,1,0:T(8,128)(2,1)}), bf16[512,8,1152]{2,1,0:T(8,128)(2,1)}, u32[]{:S(2)}, u32[]{:S(2)}) async-start(bf16[512,8,1152]{2,1,0:T(8,128)(2,1)} %stack.2), calls=%async_computation.1 | async-start | bytes 18874368 | tf_op jit(solution)/shard_map/all_to_all | solution.py:27
  289.3 1.3 copy-start.1
  294.0 0.8 copy-start.2
